TPU v7x, 512 devices: a whole 4x4x16 slice. The times are simulated.
512 devices in a mesh: gx: 32 (over x, y, core), gy: 16 (over z).
Axes of the slice: x: 4, y: 4, z: 16, core: 2. Of those that a mesh axis runs over, the one named last changes fastest.
Arguments:
- right_side: float32 [2, 512, 2048], P(None, 'gx', 'gy'), may hold values from -160 to 160
- conductivity: float32 [512, 2048], P('gx', 'gy'), may hold values from 0.2 to 5
- leaf_inverse: float32 [128, 64, 128, 128], P('gx', 'gy'), may hold values from -1 to 4, as said below
- front_basis: float32 [512, 2048, 128], P('gx', 'gy'), may hold values from -0.25 to 0.25
- leaf_transfer: float32 [32, 16, 128, 128], P('gx', 'gy'), may hold values from -0.4375 to 0.4375
- node_transfer: float32 [32, 16, 8, 128, 128], P('gx', 'gy'), may hold values from -1 to 1, as said below
- leaf_front: float32 [32, 16, 128, 128], P('gx', 'gy'), may hold values from -1 to 1, as said below
- node_front: float32 [32, 16, 9, 128, 128], P('gx', 'gy'), may hold values from -1 to 1, as said below
Outputs:
- solution: float32 [2, 512, 2048], P(None, 'gx', 'gy')
- residual: float32 [2, 512, 2048], P(None, 'gx', 'gy')
- direction: float32 [2, 512, 2048], P(None, 'gx', 'gy')
Inputs may be any that keep to these rules, and one draw needn't show every extreme that they name: `leaf_inverse`: every block is symmetric and positive definite. `leaf_front`: every matrix is symmetric and positive definite. `node_front`: every matrix is symmetric and positive definite; entry h - 1 is the same for all tiles covered by one node of level h. `node_transfer`: entry h - 1 is the same for all tiles covered by one node of level h.
All inputs are finite; a program needn't handle non-finite values.
Results may differ from a plain program's by a relative error of at most 0.0001.
Values sent between devices are 32-bit elements; how exact they have to be, the bound alone decides.
A program may use at most 64 MiB of HBM per device.

v0:
```python
from functools import partial
import jax
import jax.numpy as jnp
from jax import lax
from jax.sharding import PartitionSpec as P

LBX = 4
LBY = 32
HIGHEST = lax.Precision.HIGHEST


def extended(cells, sides, width):
    for axis, dim in sides:
        count = lax.axis_size(axis)
        ends = count - 1
        head = lax.slice_in_dim(cells, 0, width, axis=dim)
        tail = lax.slice_in_dim(cells, cells.shape[dim] - width, cells.shape[dim], axis=dim)
        cells = jnp.concatenate(
            [
                lax.ppermute(tail, axis, [(i, (i + 1) % count) for i in range(ends)]),
                cells,
                lax.ppermute(head, axis, [((i + 1) % count, i) for i in range(ends)]),
            ],
            axis=dim,
        )
    return cells


def from_partner(value, axis, distance):
    mask = 2**distance
    pairs = [(source, source ^ mask) for source in range(lax.axis_size(axis))]
    return lax.ppermute(value, axis, pairs)


def operate_padded(padded, padded_k):
    extent_x = padded.shape[1] - 2
    extent_y = padded.shape[2] - 2
    center = padded[:, 1:-1, 1:-1]
    center_k = padded_k[1:-1, 1:-1]
    summed = jnp.zeros_like(center)
    for offset_x, offset_y in ((2, 1), (0, 1), (1, 2), (1, 0)):
        beside = padded[:, offset_x : offset_x + extent_x, offset_y : offset_y + extent_y]
        beside_k = padded_k[offset_x : offset_x + extent_x, offset_y : offset_y + extent_y]
        summed = summed + 0.5 * (center_k + beside_k) * (center - beside)
    return summed


def stencil(values, conductivity):
    stacked = jnp.concatenate([values, conductivity[None]], axis=0)
    padded = extended(stacked, (("gx", 1), ("gy", 2)), 1)
    return operate_padded(padded[:-1], padded[-1])


def leaf_apply(values, leaf_inverse):
    count_s, extent_x, extent_y = values.shape
    blocks_x = extent_x // LBX
    blocks_y = extent_y // LBY
    grouped = values.reshape(count_s, blocks_x, LBX, blocks_y, LBY).transpose(0, 1, 3, 2, 4)
    grouped = grouped.reshape(count_s, blocks_x, blocks_y, LBX * LBY)
    mapped = jnp.einsum("xyij,sxyj->sxyi", leaf_inverse, grouped, precision=HIGHEST)
    mapped = mapped.reshape(count_s, blocks_x, blocks_y, LBX, LBY).transpose(0, 1, 3, 2, 4)
    return mapped.reshape(count_s, extent_x, extent_y)


def spread_tree(coeffs, leaf_transfer, node_transfer, leaf_front, node_front):
    levels = lax.axis_size(("gx", "gy")).bit_length() - 1
    leaf_t = leaf_transfer[0, 0]
    leaf_f = leaf_front[0, 0]
    node_t = node_transfer[0, 0]
    node_f = node_front[0, 0]
    uppers = [coeffs]
    moving = jnp.dot(coeffs, leaf_t, precision=HIGHEST)
    for height in range(1, levels + 1):
        partner = from_partner(moving, ("gx", "gy"), height - 1)
        summed = moving + partner
        uppers.append(summed)
        if height < levels:
            moving = jnp.dot(summed, node_t[height - 1], precision=HIGHEST)
    downward = jnp.dot(uppers[levels], node_f[levels - 1], precision=HIGHEST)
    for height in range(levels, 1, -1):
        downward = jnp.dot(downward, node_t[height - 2].T, precision=HIGHEST) + jnp.dot(
            uppers[height - 1], node_f[height - 2], precision=HIGHEST
        )
    return jnp.dot(downward, leaf_t.T, precision=HIGHEST) + jnp.dot(
        coeffs, leaf_f, precision=HIGHEST
    )


def precondition(
    values, leaf_inverse, front_basis, leaf_transfer, node_transfer, leaf_front, node_front
):
    near = leaf_apply(values, leaf_inverse)
    coeffs = jnp.einsum("sab,abk->sk", values, front_basis, precision=HIGHEST)
    spread = spread_tree(coeffs, leaf_transfer, node_transfer, leaf_front, node_front)
    return near + jnp.einsum("sk,abk->sab", spread, front_basis, precision=HIGHEST)


def on_device(
    right_side,
    conductivity,
    leaf_inverse,
    front_basis,
    leaf_transfer,
    node_transfer,
    leaf_front,
    node_front,
):
    apply_inverse = partial(
        precondition,
        leaf_inverse=leaf_inverse,
        front_basis=front_basis,
        leaf_transfer=leaf_transfer,
        node_transfer=node_transfer,
        leaf_front=leaf_front,
        node_front=node_front,
    )
    first_z = apply_inverse(right_side)
    local_rz = jnp.sum(right_side * first_z, axis=(1, 2))
    rz_old = lax.psum(local_rz, ("gx", "gy"))
    applied = stencil(first_z, conductivity)
    curvature = lax.psum(jnp.sum(first_z * applied, axis=(1, 2)), ("gx", "gy"))
    step_size = (rz_old / curvature)[:, None, None]
    solution = step_size * first_z
    residual = right_side - step_size * applied
    second_z = apply_inverse(residual)
    rz_new = lax.psum(jnp.sum(residual * second_z, axis=(1, 2)), ("gx", "gy"))
    direction = second_z + (rz_new / rz_old)[:, None, None] * first_z
    return (solution, residual, direction)


def solution(mesh):
    return jax.shard_map(
        on_device,
        mesh=mesh,
        in_specs=(
            P(None, "gx", "gy"),
            P("gx", "gy"),
            P("gx", "gy", None, None),
            P("gx", "gy", None),
            P("gx", "gy", None, None),
            P("gx", "gy", None, None, None),
            P("gx", "gy", None, None),
            P("gx", "gy", None, None, None),
        ),
        out_specs=(P(None, "gx", "gy"), P(None, "gx", "gy"), P(None, "gx", "gy")),
        check_vma=False,
    )
```

profile of v0, /device:TPU:1, one launch (start us, length us, event | category | flops | bytes accessed | tf_op | source)
XLA Modules:
  0.0 377.9 jit_solution(12129984315452648051)
XLA Ops:
  0.7 1.2 copy-done
  1.9 1.3 convolution_bitcast_fusion.3
  3.4 4.4 %collective-permute-start = (f32[2,128]{1,0:T(2,128)S(1)}, f32[2,128]{1,0:T(2,128)S(1)}, u32[]{:S(2)}, u32[]{:S(2)}) collective-permute-start(f32[2,128]{1,0:T(2,128)S(1)} %fusion.94), channel_id=1, source_target_pairs={{0,1},{1,0},{2,3},{3,2},{4,5},{5,4},{6,7},{7,6},{8,9},{9,8},{10,11... | collective-permute-start | bytes 3080 | tf_op jit(solution)/shard_map/ppermute | solution.py:32
  7.7 0.9 collective-permute-done
  8.8 4.9 %collective-permute-start.1 = (f32[2,128]{1,0:T(2,128)S(1)}, f32[2,128]{1,0:T(2,128)S(1)}, u32[]{:S(2)}, u32[]{:S(2)}) collective-permute-start(f32[2,128]{1,0:T(2,128)S(1)} %fusion.86), channel_id=1, source_target_pairs={{0,2},{1,3},{2,0},{3,1},{4,6},{5,7},{6,4},{7,5},{8,10},{9,11},{10,... | collective-permute-start | bytes 3080 | tf_op jit(solution)/shard_map/ppermute | solution.py:32
  13.8 0.9 collective-permute-done.1
  14.9 8.8 %collective-permute-start.2 = (f32[2,128]{1,0:T(2,128)S(1)}, f32[2,128]{1,0:T(2,128)S(1)}, u32[]{:S(2)}, u32[]{:S(2)}) collective-permute-start(f32[2,128]{1,0:T(2,128)S(1)} %fusion.78), channel_id=1, source_target_pairs={{0,4},{1,5},{2,6},{3,7},{4,0},{5,1},{6,2},{7,3},{8,12},{9,13},{10,... | collective-permute-start | bytes 3080 | tf_op jit(solution)/shard_map/ppermute | solution.py:32
  23.7 0.9 collective-permute-done.2
  24.8 13.1 %collective-permute-start.3 = (f32[2,128]{1,0:T(2,128)S(1)}, f32[2,128]{1,0:T(2,128)S(1)}, u32[]{:S(2)}, u32[]{:S(2)}) collective-permute-start(f32[2,128]{1,0:T(2,128)S(1)} %fusion.70), channel_id=1, source_target_pairs={{0,8},{1,9},{2,10},{3,11},{4,12},{5,13},{6,14},{7,15},{8,0},{9,1},... | collective-permute-start | bytes 3080 | tf_op jit(solution)/shard_map/ppermute | solution.py:32
  37.9 0.9 collective-permute-done.3
  39.0 9.2 %collective-permute-start.4 = (f32[2,128]{1,0:T(2,128)S(1)}, f32[2,128]{1,0:T(2,128)S(1)}, u32[]{:S(2)}, u32[]{:S(2)}) collective-permute-start(f32[2,128]{1,0:T(2,128)S(1)} %fusion.62), channel_id=1, source_target_pairs={{0,16},{1,17},{2,18},{3,19},{4,20},{5,21},{6,22},{7,23},{8,24},{9,... | collective-permute-start | bytes 3080 | tf_op jit(solution)/shard_map/ppermute | solution.py:32
  48.2 0.8 collective-permute-done.4
  49.1 1.9 collective-permute-start.5
  51.1 2.4 collective-permute-done.5
  53.6 2.5 collective-permute-start.6
  56.2 3.3 collective-permute-done.6
  59.6 1.9 collective-permute-start.7
  61.5 0.8 reshape.70
  62.5 1.4 collective-permute-done.7
  64.1 2.5 collective-permute-start.8
  66.6 1.7 convolution_bitcast_fusion.1
  68.6 1.4 collective-permute-done.8
  73.5 0.5 copy-done.6
  74.2 1.0 convolution_add_fusion.1
  75.2 6.8 %collective-permute-start.10 = (f32[3,1,128]{2,0,1:T(4,128)S(1)}, f32[3,1,128]{2,0,1:T(4,128)S(1)}, u32[]{:S(2)}, u32[]{:S(2)}) collective-permute-start(f32[3,1,128]{2,0,1:T(4,128)S(1)} %get-tuple-element.18), channel_id=1, source_target_pairs={{16,0},{32,16},{48,32},{64,48},{80,64},{96,80},{112,96},{128,112},... | collective-permute-start | bytes 4616 | tf_op jit(solution)/shard_map/ppermute | solution.py:22
  82.0 1.9 collective-permute-start.9
  83.9 1.1 collective-permute-done.9
  85.2 1.6 collective-permute-start.11
  86.8 1.3 collective-permute-start.12
  88.1 3.4 collective-permute-done.12
  91.8 0.6 copy-done.5
  92.7 109.6 %all-reduce = (f32[2]{0:T(128)S(1)}, f32[2]{0:T(128)S(1)}) all-reduce(f32[2]{0:T(128)S(1)} %get-tuple-element.7, f32[2]{0:T(128)S(1)} %get-tuple-element.6), channel_id=1, replica_groups=mesh['gx'=32,'gy'=16] {'gx','gy'}, use_global_device_ids=true, to_apply=%region_1.0 | all-reduce | flops 4 | bytes 32 | tf_op jit(solution)/shard_map/psum | solution.py:119
  202.3 0.6 copy-done.18
  202.9 0.5 copy-done.16
  203.5 0.6 convolution_bitcast_fusion.2
  204.2 1.9 collective-permute-start.13
  206.2 2.4 collective-permute-done.13
  208.7 1.9 collective-permute-start.14
  210.6 3.3 collective-permute-done.14
  214.1 4.0 %collective-permute-start.15 = (f32[2,128]{1,0:T(2,128)S(1)}, f32[2,128]{1,0:T(2,128)S(1)}, u32[]{:S(2)}, u32[]{:S(2)}) collective-permute-start(f32[2,128]{1,0:T(2,128)S(1)} %fusion.74), channel_id=1, source_target_pairs={{0,4},{1,5},{2,6},{3,7},{4,0},{5,1},{6,2},{7,3},{8,12},{9,13},{10,... | collective-permute-start | bytes 3080 | tf_op jit(solution)/shard_map/ppermute | solution.py:32
  218.1 4.2 %collective-permute-done.15 = f32[2,128]{1,0:T(2,128)S(1)} collective-permute-done((f32[2,128]{1,0:T(2,128)S(1)}, f32[2,128]{1,0:T(2,128)S(1)}, u32[]{:S(2)}, u32[]{:S(2)}) %collective-permute-start.15) | collective-permute-done | bytes 1056 | tf_op jit(solution)/shard_map/ppermute | solution.py:32
  222.5 8.2 %collective-permute-start.16 = (f32[2,128]{1,0:T(2,128)S(1)}, f32[2,128]{1,0:T(2,128)S(1)}, u32[]{:S(2)}, u32[]{:S(2)}) collective-permute-start(f32[2,128]{1,0:T(2,128)S(1)} %fusion.66), channel_id=1, source_target_pairs={{0,8},{1,9},{2,10},{3,11},{4,12},{5,13},{6,14},{7,15},{8,0},{9,1},... | collective-permute-start | bytes 3080 | tf_op jit(solution)/shard_map/ppermute | solution.py:32
  230.7 4.8 %collective-permute-done.16 = f32[2,128]{1,0:T(2,128)S(1)} collective-permute-done((f32[2,128]{1,0:T(2,128)S(1)}, f32[2,128]{1,0:T(2,128)S(1)}, u32[]{:S(2)}, u32[]{:S(2)}) %collective-permute-start.16) | collective-permute-done | bytes 1056 | tf_op jit(solution)/shard_map/ppermute | solution.py:32
  236.0 7.7 %collective-permute-start.17 = (f32[2,128]{1,0:T(2,128)S(1)}, f32[2,128]{1,0:T(2,128)S(1)}, u32[]{:S(2)}, u32[]{:S(2)}) collective-permute-start(f32[2,128]{1,0:T(2,128)S(1)} %fusion.58), channel_id=1, source_target_pairs={{0,16},{1,17},{2,18},{3,19},{4,20},{5,21},{6,22},{7,23},{8,24},{9,... | collective-permute-start | bytes 3080 | tf_op jit(solution)/shard_map/ppermute | solution.py:32
  243.7 0.8 collective-permute-done.17
  245.1 1.9 collective-permute-start.18
  247.0 2.4 collective-permute-done.18
  250.0 2.5 collective-permute-start.19
  252.5 3.3 collective-permute-done.19
  256.3 1.9 collective-permute-start.20
  258.5 2.2 collective-permute-done.20
  260.7 0.8 fusion.26
  261.6 2.8 collective-permute-start.21
  264.3 1.7 convolution_bitcast_fusion
  266.1 0.6 copy.19
  267.7 0.9 convolution_add_fusion.10
  268.8 0.5 copy-done.15
  269.6 0.5 copy-done.13
  270.5 0.5 copy-done.11
  273.5 1.1 multiply_reduce_fusion
  274.6 101.4 %psum.23 = f32[2]{0:T(128)S(1)} all-reduce(f32[2]{0:T(128)S(1)} %get-tuple-element.21), channel_id=1, replica_groups=mesh['gx'=32,'gy'=16] {'gx','gy'}, use_global_device_ids=true, to_apply=%region_5.0 | all-reduce | flops 2 | bytes 16 | tf_op jit(solution)/shard_map/psum | solution.py:126
  376.0 0.6 copy-done.17
  376.7 0.6 copy.18
  377.3 0.6 copy.20
  (110 shorter events, 13.7 us)
Async XLA Ops:
  0.6 1.2 copy-start
  0.6 2.5 copy-start.4
  0.7 8.0 %copy-start.1 = (f32[1,1,8,128,128]{4,3,2,1,0:T(8,128)S(1)}, f32[1,1,8,128,128]{4,3,2,1,0:T(8,128)}, u32[]{:S(2)}) copy-start(f32[1,1,8,128,128]{4,3,2,1,0:T(8,128)} %param.13) | copy-start | bytes 1572868
  0.7 65.9 %copy-start.2 = (f32[4,4,128,128]{3,2,1,0:T(8,128)S(1)}, f32[4,4,128,128]{3,2,1,0:T(8,128)}, u32[]{:S(2)}) copy-start(f32[4,4,128,128]{3,2,1,0:T(8,128)} %param.10) | copy-start | bytes 3145732
  3.4 5.3 %collective-permute-start = (f32[2,128]{1,0:T(2,128)S(1)}, f32[2,128]{1,0:T(2,128)S(1)}, u32[]{:S(2)}, u32[]{:S(2)}) collective-permute-start(f32[2,128]{1,0:T(2,128)S(1)} %fusion.94), channel_id=1, source_target_pairs={{0,1},{1,0},{2,3},{3,2},{4,5},{5,4},{6,7},{7,6},{8,9},{9,8},{10,11... | collective-permute-start | bytes 3080 | tf_op jit(solution)/shard_map/ppermute | solution.py:32
  8.8 5.9 %collective-permute-start.1 = (f32[2,128]{1,0:T(2,128)S(1)}, f32[2,128]{1,0:T(2,128)S(1)}, u32[]{:S(2)}, u32[]{:S(2)}) collective-permute-start(f32[2,128]{1,0:T(2,128)S(1)} %fusion.86), channel_id=1, source_target_pairs={{0,2},{1,3},{2,0},{3,1},{4,6},{5,7},{6,4},{7,5},{8,10},{9,11},{10,... | collective-permute-start | bytes 3080 | tf_op jit(solution)/shard_map/ppermute | solution.py:32
  14.9 9.8 %collective-permute-start.2 = (f32[2,128]{1,0:T(2,128)S(1)}, f32[2,128]{1,0:T(2,128)S(1)}, u32[]{:S(2)}, u32[]{:S(2)}) collective-permute-start(f32[2,128]{1,0:T(2,128)S(1)} %fusion.78), channel_id=1, source_target_pairs={{0,4},{1,5},{2,6},{3,7},{4,0},{5,1},{6,2},{7,3},{8,12},{9,13},{10,... | collective-permute-start | bytes 3080 | tf_op jit(solution)/shard_map/ppermute | solution.py:32
  24.8 14.0 %collective-permute-start.3 = (f32[2,128]{1,0:T(2,128)S(1)}, f32[2,128]{1,0:T(2,128)S(1)}, u32[]{:S(2)}, u32[]{:S(2)}) collective-permute-start(f32[2,128]{1,0:T(2,128)S(1)} %fusion.70), channel_id=1, source_target_pairs={{0,8},{1,9},{2,10},{3,11},{4,12},{5,13},{6,14},{7,15},{8,0},{9,1},... | collective-permute-start | bytes 3080 | tf_op jit(solution)/shard_map/ppermute | solution.py:32
  39.0 10.0 %collective-permute-start.4 = (f32[2,128]{1,0:T(2,128)S(1)}, f32[2,128]{1,0:T(2,128)S(1)}, u32[]{:S(2)}, u32[]{:S(2)}) collective-permute-start(f32[2,128]{1,0:T(2,128)S(1)} %fusion.62), channel_id=1, source_target_pairs={{0,16},{1,17},{2,18},{3,19},{4,20},{5,21},{6,22},{7,23},{8,24},{9,... | collective-permute-start | bytes 3080 | tf_op jit(solution)/shard_map/ppermute | solution.py:32
  49.1 4.3 %collective-permute-start.5 = (f32[2,128]{1,0:T(2,128)S(1)}, f32[2,128]{1,0:T(2,128)S(1)}, u32[]{:S(2)}, u32[]{:S(2)}) collective-permute-start(f32[2,128]{1,0:T(2,128)S(1)} %fusion.54), channel_id=1, source_target_pairs={{0,32},{1,33},{2,34},{3,35},{4,36},{5,37},{6,38},{7,39},{8,40},{9,... | collective-permute-start | bytes 3080 | tf_op jit(solution)/shard_map/ppermute | solution.py:32
  53.6 5.8 %collective-permute-start.6 = (f32[2,128]{1,0:T(2,128)S(1)}, f32[2,128]{1,0:T(2,128)S(1)}, u32[]{:S(2)}, u32[]{:S(2)}) collective-permute-start(f32[2,128]{1,0:T(2,128)S(1)} %fusion.46), channel_id=1, source_target_pairs={{0,64},{1,65},{2,66},{3,67},{4,68},{5,69},{6,70},{7,71},{8,72},{9,... | collective-permute-start | bytes 3080 | tf_op jit(solution)/shard_map/ppermute | solution.py:32
  59.6 4.3 %collective-permute-start.7 = (f32[2,128]{1,0:T(2,128)S(1)}, f32[2,128]{1,0:T(2,128)S(1)}, u32[]{:S(2)}, u32[]{:S(2)}) collective-permute-start(f32[2,128]{1,0:T(2,128)S(1)} %fusion.38), channel_id=1, source_target_pairs={{0,128},{1,129},{2,130},{3,131},{4,132},{5,133},{6,134},{7,135},{8... | collective-permute-start | bytes 3080 | tf_op jit(solution)/shard_map/ppermute | solution.py:32
  64.1 6.0 %copy-start.3 = (f32[1,1,9,128,128]{4,3,2,1,0:T(8,128)S(1)}, f32[1,1,9,128,128]{4,3,2,1,0:T(8,128)}, u32[]{:S(2)}) copy-start(f32[1,1,9,128,128]{4,3,2,1,0:T(8,128)} %param.15) | copy-start | bytes 1769476
  64.1 6.0 %collective-permute-start.8 = (f32[2,128]{1,0:T(2,128)S(1)}, f32[2,128]{1,0:T(2,128)S(1)}, u32[]{:S(2)}, u32[]{:S(2)}) collective-permute-start(f32[2,128]{1,0:T(2,128)S(1)} %fusion.30), channel_id=1, source_target_pairs={{0,256},{1,257},{2,258},{3,259},{4,260},{5,261},{6,262},{7,263},{8... | collective-permute-start | bytes 3080 | tf_op jit(solution)/shard_map/ppermute | solution.py:32
  73.1 0.9 copy-start.6
  74.2 1.0 copy-start.7
  75.2 8.8 %collective-permute-start.10 = (f32[3,1,128]{2,0,1:T(4,128)S(1)}, f32[3,1,128]{2,0,1:T(4,128)S(1)}, u32[]{:S(2)}, u32[]{:S(2)}) collective-permute-start(f32[3,1,128]{2,0,1:T(4,128)S(1)} %get-tuple-element.18), channel_id=1, source_target_pairs={{16,0},{32,16},{48,32},{64,48},{80,64},{96,80},{112,96},{128,112},... | collective-permute-start | bytes 4616 | tf_op jit(solution)/shard_map/ppermute | solution.py:22
  82.0 3.1 collective-permute-start.9
  85.2 3.0 collective-permute-start.11
  86.8 4.7 %collective-permute-start.12 = (f32[3,18,1]{2,0,1:T(4,128)S(1)}, f32[3,18,1]{2,0,1:T(4,128)S(1)}, u32[]{:S(2)}, u32[]{:S(2)}) collective-permute-start(f32[3,18,1]{2,0,1:T(4,128)S(1)} %get-tuple-element.11), channel_id=1, source_target_pairs={{1,0},{2,1},{3,2},{4,3},{5,4},{6,5},{7,6},{8,7},{9,8},{10,9},{11,1... | collective-permute-start | bytes 656 | tf_op jit(solution)/shard_map/ppermute | solution.py:22
  91.7 0.7 copy-start.5
  202.3 0.6 copy-start.18
  202.9 0.5 copy-start.16
  204.2 4.3 %collective-permute-start.13 = (f32[2,128]{1,0:T(2,128)S(1)}, f32[2,128]{1,0:T(2,128)S(1)}, u32[]{:S(2)}, u32[]{:S(2)}) collective-permute-start(f32[2,128]{1,0:T(2,128)S(1)} %fusion.90), channel_id=1, source_target_pairs={{0,1},{1,0},{2,3},{3,2},{4,5},{5,4},{6,7},{7,6},{8,9},{9,8},{10,11... | collective-permute-start | bytes 3080 | tf_op jit(solution)/shard_map/ppermute | solution.py:32
  208.7 5.2 %collective-permute-start.14 = (f32[2,128]{1,0:T(2,128)S(1)}, f32[2,128]{1,0:T(2,128)S(1)}, u32[]{:S(2)}, u32[]{:S(2)}) collective-permute-start(f32[2,128]{1,0:T(2,128)S(1)} %fusion.82), channel_id=1, source_target_pairs={{0,2},{1,3},{2,0},{3,1},{4,6},{5,7},{6,4},{7,5},{8,10},{9,11},{10,... | collective-permute-start | bytes 3080 | tf_op jit(solution)/shard_map/ppermute | solution.py:32
  214.1 8.2 %collective-permute-start.15 = (f32[2,128]{1,0:T(2,128)S(1)}, f32[2,128]{1,0:T(2,128)S(1)}, u32[]{:S(2)}, u32[]{:S(2)}) collective-permute-start(f32[2,128]{1,0:T(2,128)S(1)} %fusion.74), channel_id=1, source_target_pairs={{0,4},{1,5},{2,6},{3,7},{4,0},{5,1},{6,2},{7,3},{8,12},{9,13},{10,... | collective-permute-start | bytes 3080 | tf_op jit(solution)/shard_map/ppermute | solution.py:32
  222.5 13.0 %collective-permute-start.16 = (f32[2,128]{1,0:T(2,128)S(1)}, f32[2,128]{1,0:T(2,128)S(1)}, u32[]{:S(2)}, u32[]{:S(2)}) collective-permute-start(f32[2,128]{1,0:T(2,128)S(1)} %fusion.66), channel_id=1, source_target_pairs={{0,8},{1,9},{2,10},{3,11},{4,12},{5,13},{6,14},{7,15},{8,0},{9,1},... | collective-permute-start | bytes 3080 | tf_op jit(solution)/shard_map/ppermute | solution.py:32
  235.5 0.5 copy-start.8
  236.0 8.5 %collective-permute-start.17 = (f32[2,128]{1,0:T(2,128)S(1)}, f32[2,128]{1,0:T(2,128)S(1)}, u32[]{:S(2)}, u32[]{:S(2)}) collective-permute-start(f32[2,128]{1,0:T(2,128)S(1)} %fusion.58), channel_id=1, source_target_pairs={{0,16},{1,17},{2,18},{3,19},{4,20},{5,21},{6,22},{7,23},{8,24},{9,... | collective-permute-start | bytes 3080 | tf_op jit(solution)/shard_map/ppermute | solution.py:32
  244.5 0.6 copy-start.10
  245.1 4.3 %collective-permute-start.18 = (f32[2,128]{1,0:T(2,128)S(1)}, f32[2,128]{1,0:T(2,128)S(1)}, u32[]{:S(2)}, u32[]{:S(2)}) collective-permute-start(f32[2,128]{1,0:T(2,128)S(1)} %fusion.50), channel_id=1, source_target_pairs={{0,32},{1,33},{2,34},{3,35},{4,36},{5,37},{6,38},{7,39},{8,40},{9,... | collective-permute-start | bytes 3080 | tf_op jit(solution)/shard_map/ppermute | solution.py:32
  249.4 0.6 copy-start.12
  250.0 5.8 %collective-permute-start.19 = (f32[2,128]{1,0:T(2,128)S(1)}, f32[2,128]{1,0:T(2,128)S(1)}, u32[]{:S(2)}, u32[]{:S(2)}) collective-permute-start(f32[2,128]{1,0:T(2,128)S(1)} %fusion.42), channel_id=1, source_target_pairs={{0,64},{1,65},{2,66},{3,67},{4,68},{5,69},{6,70},{7,71},{8,72},{9,... | collective-permute-start | bytes 3080 | tf_op jit(solution)/shard_map/ppermute | solution.py:32
  255.8 0.6 copy-start.14
  256.3 4.4 %collective-permute-start.20 = (f32[2,128]{1,0:T(2,128)S(1)}, f32[2,128]{1,0:T(2,128)}, u32[]{:S(2)}, u32[]{:S(2)}) collective-permute-start(f32[2,128]{1,0:T(2,128)S(1)} %fusion.34), channel_id=1, source_target_pairs={{0,128},{1,129},{2,130},{3,131},{4,132},{5,133},{6,134},{7,135},{8... | collective-permute-start | bytes 3080 | tf_op jit(solution)/shard_map/ppermute | solution.py:32
  261.6 5.8 %collective-permute-start.21 = (f32[2,128]{1,0:T(2,128)S(1)}, f32[2,128]{1,0:T(2,128)S(1)}, u32[]{:S(2)}, u32[]{:S(2)}) collective-permute-start(f32[2,128]{1,0:T(2,128)S(1)} %fusion.26), channel_id=1, source_target_pairs={{0,256},{1,257},{2,258},{3,259},{4,260},{5,261},{6,262},{7,263},{8... | collective-permute-start | bytes 3080 | tf_op jit(solution)/shard_map/ppermute | solution.py:32
  268.6 0.7 copy-start.15
  269.4 0.7 copy-start.13
  270.3 0.7 copy-start.11
  271.1 0.7 copy-start.9
  274.6 101.4 %copy-start.19 = (f32[2]{0:T(128)S(1)}, f32[2]{0:T(128)}, u32[]{:S(2)}) copy-start(f32[2]{0:T(128)} %copy-done.18) | copy-start | bytes 28
  376.0 0.6 copy-start.17
where the time goes:
time: 379 us; the launch traced here: 378 us
  blocking collectives  211 us (56%)
  starting transfers between devices  93.8 us (25%)
  waiting for transfers between devices  41.5 us (11%)
  matrix products  18.7 us (5%)
  local copies, waits for them, and re-layouts  11.2 us (3%)
    psum x1, blocking collectives, on_device(): rz_old = lax.psum(local_rz, ('gx', 'gy'))  110 us
    psum x1, blocking collectives, on_device(): rz_new = lax.psum(jnp.sum(residual * second_z, axis=(1, 2)), ('gx', 'gy'))  101 us
    ppermute x18, starting transfers between devices, from_partner(): return lax.ppermute(value, axis, pairs)  82.1 us
    ppermute x18, waiting for transfers between devices, from_partner(): return lax.ppermute(value, axis, pairs)  37 us
    unnamed x44, local copies, waits for them, and re-layouts  9.48 us
    ppermute x2, starting transfers between devices, extended(): lax.ppermute(head, axis, [((i + 1) % count, i) for i in range(ends)])  8.12 us
  transfers between devices with their start and end apart: 22, of which 20 were waited for; matrix products, arithmetic and copies ran while one was open for 2% of the time, Pallas kernels for 0%

commit v1 on v0

--- a/solution.py
+++ b/solution.py
@@ -116,7 +116,8 @@
     )
     first_z = apply_inverse(right_side)
     local_rz = jnp.sum(right_side * first_z, axis=(1, 2))
-    rz_old = lax.psum(local_rz, ("gx", "gy"))
+    inner = lax.psum(local_rz, "gx")
+    rz_old = lax.psum(inner, "gy")
     applied = stencil(first_z, conductivity)
     curvature = lax.psum(jnp.sum(first_z * applied, axis=(1, 2)), ("gx", "gy"))
     step_size = (rz_old / curvature)[:, None, None]

time: 379 us -> 470 us (1.24)
  blocking collectives: 211 us -> 301 us
  starting transfers between devices: 93.8 us -> 104 us
  waiting for transfers between devices: 41.5 us -> 31.9 us
    psum x1 -> x3, blocking collectives: 110 us -> 197 us  [the longest x1 106 us: on_device(): curvature = lax.psum(jnp.sum(first_z * applied, axis=(1, 2)), ('gx', 'gy'))]
    ppermute x18, starting transfers between devices: 82.1 us -> 92.4 us  [from_partner(): return lax.ppermute(value, axis, pairs)]
    ppermute x18, waiting for transfers between devices: 37 us -> 27.4 us  [from_partner(): return lax.ppermute(value, axis, pairs)]
  transfers between devices with their start and end apart: 22 -> 22, of which waited for: 20 -> 19; matrix products, arithmetic and copies ran while one was open for 2% -> 1% of each run, Pallas kernels for 0% -> 0%
where the time goes in v1:
time: 470 us; the launch traced here: 469 us
  blocking collectives  301 us (64%)
  starting transfers between devices  104 us (22%)
  waiting for transfers between devices  31.9 us (7%)
  matrix products  18.6 us (4%)
  local copies, waits for them, and re-layouts  10.9 us (2%)
    psum x1, blocking collectives, on_device(): curvature = lax.psum(jnp.sum(first_z * applied, axis=(1, 2)), ('gx', 'gy'))  106 us
    psum x1, blocking collectives, on_device(): rz_new = lax.psum(jnp.sum(residual * second_z, axis=(1, 2)), ('gx', 'gy'))  105 us
    ppermute x18, starting transfers between devices, from_partner(): return lax.ppermute(value, axis, pairs)  92.4 us
    psum x1, blocking collectives, on_device(): inner = lax.psum(local_rz, 'gx')  64.3 us
    ppermute x18, waiting for transfers between devices, from_partner(): return lax.ppermute(value, axis, pairs)  27.4 us
    psum x1, blocking collectives, on_device(): rz_old = lax.psum(inner, 'gy')  26.4 us
  transfers between devices with their start and end apart: 22, of which 19 were waited for; matrix products, arithmetic and copies ran while one was open for 1% of the time, Pallas kernels for 0%

profile of v1, /device:TPU:1, one launch (start us, length us, event | category | flops | bytes accessed | tf_op | source)
XLA Modules:
  0.0 468.6 jit_solution(5560506469664577124)
XLA Ops:
  0.7 1.2 copy-done
  1.9 1.3 convolution_bitcast_fusion.3
  3.4 4.4 collective-permute-start
  7.7 0.9 collective-permute-done
  8.8 4.9 %collective-permute-start.1 = (f32[2,128]{1,0:T(2,128)S(1)}, f32[2,128]{1,0:T(2,128)S(1)}, u32[]{:S(2)}, u32[]{:S(2)}) collective-permute-start(f32[2,128]{1,0:T(2,128)S(1)} %fusion.86), channel_id=1, source_target_pairs={{0,2},{1,3},{2,0},{3,1},{4,6},{5,7},{6,4},{7,5},{8,10},{9,11},{10,... | collective-permute-start | bytes 3080 | tf_op jit(solution)/shard_map/ppermute | solution.py:32
  13.8 0.9 collective-permute-done.1
  14.9 8.8 %collective-permute-start.2 = (f32[2,128]{1,0:T(2,128)S(1)}, f32[2,128]{1,0:T(2,128)S(1)}, u32[]{:S(2)}, u32[]{:S(2)}) collective-permute-start(f32[2,128]{1,0:T(2,128)S(1)} %fusion.78), channel_id=1, source_target_pairs={{0,4},{1,5},{2,6},{3,7},{4,0},{5,1},{6,2},{7,3},{8,12},{9,13},{10,... | collective-permute-start | bytes 3080 | tf_op jit(solution)/shard_map/ppermute | solution.py:32
  23.7 0.9 collective-permute-done.2
  24.8 13.1 %collective-permute-start.3 = (f32[2,128]{1,0:T(2,128)S(1)}, f32[2,128]{1,0:T(2,128)S(1)}, u32[]{:S(2)}, u32[]{:S(2)}) collective-permute-start(f32[2,128]{1,0:T(2,128)S(1)} %fusion.70), channel_id=1, source_target_pairs={{0,8},{1,9},{2,10},{3,11},{4,12},{5,13},{6,14},{7,15},{8,0},{9,1},... | collective-permute-start | bytes 3080 | tf_op jit(solution)/shard_map/ppermute | solution.py:32
  37.9 0.9 collective-permute-done.3
  39.0 9.2 %collective-permute-start.4 = (f32[2,128]{1,0:T(2,128)S(1)}, f32[2,128]{1,0:T(2,128)S(1)}, u32[]{:S(2)}, u32[]{:S(2)}) collective-permute-start(f32[2,128]{1,0:T(2,128)S(1)} %fusion.62), channel_id=1, source_target_pairs={{0,16},{1,17},{2,18},{3,19},{4,20},{5,21},{6,22},{7,23},{8,24},{9,... | collective-permute-start | bytes 3080 | tf_op jit(solution)/shard_map/ppermute | solution.py:32
  48.2 0.8 collective-permute-done.4
  49.1 1.9 collective-permute-start.5
  51.1 2.4 collective-permute-done.5
  53.6 2.5 collective-permute-start.6
  56.2 3.3 collective-permute-done.6
  59.6 1.9 collective-permute-start.7
  61.5 0.8 reshape.70
  62.5 1.4 collective-permute-done.7
  64.1 2.5 collective-permute-start.8
  66.6 1.7 convolution_bitcast_fusion.1
  68.6 1.4 collective-permute-done.8
  74.2 1.0 convolution_add_fusion.1
  75.2 6.8 %collective-permute-start.10 = (f32[3,1,128]{2,0,1:T(4,128)S(1)}, f32[3,1,128]{2,0,1:T(4,128)S(1)}, u32[]{:S(2)}, u32[]{:S(2)}) collective-permute-start(f32[3,1,128]{2,0,1:T(4,128)S(1)} %get-tuple-element.16), channel_id=1, source_target_pairs={{16,0},{32,16},{48,32},{64,48},{80,64},{96,80},{112,96},{128,112},... | collective-permute-start | bytes 4616 | tf_op jit(solution)/shard_map/ppermute | solution.py:22
  82.0 1.9 collective-permute-start.9
  83.9 1.1 collective-permute-done.9
  85.2 1.6 collective-permute-start.11
  86.8 1.3 collective-permute-start.12
  88.1 3.4 collective-permute-done.12
  91.8 0.6 copy-done.5
  92.7 64.3 %psum.28 = f32[2]{0:T(128)S(1)} all-reduce(f32[2]{0:T(128)S(1)} %get-tuple-element.7), channel_id=1, replica_groups=mesh['gx'=32,'gy'=16] {'gx'}, use_global_device_ids=true, to_apply=%region_1.0 | all-reduce | flops 2 | bytes 16 | tf_op jit(solution)/shard_map/psum | solution.py:119
  157.0 26.4 %psum.29 = f32[2]{0:T(128)S(1)} all-reduce(f32[2]{0:T(128)S(1)} %psum.28), channel_id=1, replica_groups=mesh['gx'=32,'gy'=16] {'gy'}, use_global_device_ids=true, to_apply=%region_2.0 | all-reduce | flops 2 | bytes 16 | tf_op jit(solution)/shard_map/psum | solution.py:120
  183.4 105.9 %psum.30 = f32[2]{0:T(128)S(1)} all-reduce(f32[2]{0:T(128)S(1)} %get-tuple-element.6), channel_id=1, replica_groups=mesh['gx'=32,'gy'=16] {'gx','gy'}, use_global_device_ids=true, to_apply=%region_4.0 | all-reduce | flops 2 | bytes 16 | tf_op jit(solution)/shard_map/psum | solution.py:122
  289.3 0.6 copy-done.16
  290.0 0.6 convolution_bitcast_fusion.2
  290.7 3.7 collective-permute-start.13
  294.5 0.9 collective-permute-done.13
  295.6 3.0 collective-permute-start.14
  298.6 2.2 collective-permute-done.14
  300.9 5.2 %collective-permute-start.15 = (f32[2,128]{1,0:T(2,128)S(1)}, f32[2,128]{1,0:T(2,128)S(1)}, u32[]{:S(2)}, u32[]{:S(2)}) collective-permute-start(f32[2,128]{1,0:T(2,128)S(1)} %fusion.74), channel_id=1, source_target_pairs={{0,4},{1,5},{2,6},{3,7},{4,0},{5,1},{6,2},{7,3},{8,12},{9,13},{10,... | collective-permute-start | bytes 3080 | tf_op jit(solution)/shard_map/ppermute | solution.py:32
  306.1 3.1 collective-permute-done.15
  309.3 9.3 %collective-permute-start.16 = (f32[2,128]{1,0:T(2,128)S(1)}, f32[2,128]{1,0:T(2,128)S(1)}, u32[]{:S(2)}, u32[]{:S(2)}) collective-permute-start(f32[2,128]{1,0:T(2,128)S(1)} %fusion.66), channel_id=1, source_target_pairs={{0,8},{1,9},{2,10},{3,11},{4,12},{5,13},{6,14},{7,15},{8,0},{9,1},... | collective-permute-start | bytes 3080 | tf_op jit(solution)/shard_map/ppermute | solution.py:32
  318.7 3.7 collective-permute-done.16
  322.9 6.9 %collective-permute-start.17 = (f32[2,128]{1,0:T(2,128)S(1)}, f32[2,128]{1,0:T(2,128)S(1)}, u32[]{:S(2)}, u32[]{:S(2)}) collective-permute-start(f32[2,128]{1,0:T(2,128)S(1)} %fusion.58), channel_id=1, source_target_pairs={{0,16},{1,17},{2,18},{3,19},{4,20},{5,21},{6,22},{7,23},{8,24},{9,... | collective-permute-start | bytes 3080 | tf_op jit(solution)/shard_map/ppermute | solution.py:32
  329.8 0.8 collective-permute-done.17
  331.2 3.2 collective-permute-start.18
  334.4 1.1 collective-permute-done.18
  336.1 4.2 collective-permute-start.19
  340.3 1.6 collective-permute-done.19
  342.4 3.2 collective-permute-start.20
  345.9 0.9 collective-permute-done.20
  346.8 0.8 fusion.26
  347.6 4.4 collective-permute-start.21
  352.0 1.7 convolution_bitcast_fusion
  353.8 0.6 copy.19
  355.0 0.9 convolution_add_fusion.10
  356.0 0.5 copy-done.15
  356.9 0.5 copy-done.13
  357.7 0.5 copy-done.11
  360.8 1.1 multiply_reduce_fusion
  361.9 104.7 %psum.31 = f32[2]{0:T(128)S(1)} all-reduce(f32[2]{0:T(128)S(1)} %get-tuple-element.19), channel_id=1, replica_groups=mesh['gx'=32,'gy'=16] {'gx','gy'}, use_global_device_ids=true, to_apply=%region_6.0 | all-reduce | flops 2 | bytes 16 | tf_op jit(solution)/shard_map/psum | solution.py:127
  466.6 0.7 copy-done.17
  467.4 0.6 copy.18
  468.0 0.6 copy.20
  (112 shorter events, 13.9 us)
Async XLA Ops:
  0.6 1.2 copy-start
  0.6 2.5 copy-start.4
  0.7 8.0 %copy-start.1 = (f32[1,1,8,128,128]{4,3,2,1,0:T(8,128)S(1)}, f32[1,1,8,128,128]{4,3,2,1,0:T(8,128)}, u32[]{:S(2)}) copy-start(f32[1,1,8,128,128]{4,3,2,1,0:T(8,128)} %param.13) | copy-start | bytes 1572868
  0.7 65.9 %copy-start.2 = (f32[4,4,128,128]{3,2,1,0:T(8,128)S(1)}, f32[4,4,128,128]{3,2,1,0:T(8,128)}, u32[]{:S(2)}) copy-start(f32[4,4,128,128]{3,2,1,0:T(8,128)} %param.10) | copy-start | bytes 3145732
  3.4 5.3 %collective-permute-start = (f32[2,128]{1,0:T(2,128)S(1)}, f32[2,128]{1,0:T(2,128)S(1)}, u32[]{:S(2)}, u32[]{:S(2)}) collective-permute-start(f32[2,128]{1,0:T(2,128)S(1)} %fusion.94), channel_id=1, source_target_pairs={{0,1},{1,0},{2,3},{3,2},{4,5},{5,4},{6,7},{7,6},{8,9},{9,8},{10,11... | collective-permute-start | bytes 3080 | tf_op jit(solution)/shard_map/ppermute | solution.py:32
  8.8 5.9 %collective-permute-start.1 = (f32[2,128]{1,0:T(2,128)S(1)}, f32[2,128]{1,0:T(2,128)S(1)}, u32[]{:S(2)}, u32[]{:S(2)}) collective-permute-start(f32[2,128]{1,0:T(2,128)S(1)} %fusion.86), channel_id=1, source_target_pairs={{0,2},{1,3},{2,0},{3,1},{4,6},{5,7},{6,4},{7,5},{8,10},{9,11},{10,... | collective-permute-start | bytes 3080 | tf_op jit(solution)/shard_map/ppermute | solution.py:32
  14.9 9.8 %collective-permute-start.2 = (f32[2,128]{1,0:T(2,128)S(1)}, f32[2,128]{1,0:T(2,128)S(1)}, u32[]{:S(2)}, u32[]{:S(2)}) collective-permute-start(f32[2,128]{1,0:T(2,128)S(1)} %fusion.78), channel_id=1, source_target_pairs={{0,4},{1,5},{2,6},{3,7},{4,0},{5,1},{6,2},{7,3},{8,12},{9,13},{10,... | collective-permute-start | bytes 3080 | tf_op jit(solution)/shard_map/ppermute | solution.py:32
  24.8 14.0 %collective-permute-start.3 = (f32[2,128]{1,0:T(2,128)S(1)}, f32[2,128]{1,0:T(2,128)S(1)}, u32[]{:S(2)}, u32[]{:S(2)}) collective-permute-start(f32[2,128]{1,0:T(2,128)S(1)} %fusion.70), channel_id=1, source_target_pairs={{0,8},{1,9},{2,10},{3,11},{4,12},{5,13},{6,14},{7,15},{8,0},{9,1},... | collective-permute-start | bytes 3080 | tf_op jit(solution)/shard_map/ppermute | solution.py:32
  39.0 10.0 %collective-permute-start.4 = (f32[2,128]{1,0:T(2,128)S(1)}, f32[2,128]{1,0:T(2,128)S(1)}, u32[]{:S(2)}, u32[]{:S(2)}) collective-permute-start(f32[2,128]{1,0:T(2,128)S(1)} %fusion.62), channel_id=1, source_target_pairs={{0,16},{1,17},{2,18},{3,19},{4,20},{5,21},{6,22},{7,23},{8,24},{9,... | collective-permute-start | bytes 3080 | tf_op jit(solution)/shard_map/ppermute | solution.py:32
  49.1 4.3 collective-permute-start.5
  53.6 5.8 %collective-permute-start.6 = (f32[2,128]{1,0:T(2,128)S(1)}, f32[2,128]{1,0:T(2,128)S(1)}, u32[]{:S(2)}, u32[]{:S(2)}) collective-permute-start(f32[2,128]{1,0:T(2,128)S(1)} %fusion.46), channel_id=1, source_target_pairs={{0,64},{1,65},{2,66},{3,67},{4,68},{5,69},{6,70},{7,71},{8,72},{9,... | collective-permute-start | bytes 3080 | tf_op jit(solution)/shard_map/ppermute | solution.py:32
  59.6 4.3 collective-permute-start.7
  64.1 6.0 %copy-start.3 = (f32[1,1,9,128,128]{4,3,2,1,0:T(8,128)S(1)}, f32[1,1,9,128,128]{4,3,2,1,0:T(8,128)}, u32[]{:S(2)}) copy-start(f32[1,1,9,128,128]{4,3,2,1,0:T(8,128)} %param.15) | copy-start | bytes 1769476
  64.1 6.0 %collective-permute-start.8 = (f32[2,128]{1,0:T(2,128)S(1)}, f32[2,128]{1,0:T(2,128)S(1)}, u32[]{:S(2)}, u32[]{:S(2)}) collective-permute-start(f32[2,128]{1,0:T(2,128)S(1)} %fusion.30), channel_id=1, source_target_pairs={{0,256},{1,257},{2,258},{3,259},{4,260},{5,261},{6,262},{7,263},{8... | collective-permute-start | bytes 3080 | tf_op jit(solution)/shard_map/ppermute | solution.py:32
  73.1 0.9 copy-start.6
  74.2 1.0 copy-start.7
  75.2 8.8 %collective-permute-start.10 = (f32[3,1,128]{2,0,1:T(4,128)S(1)}, f32[3,1,128]{2,0,1:T(4,128)S(1)}, u32[]{:S(2)}, u32[]{:S(2)}) collective-permute-start(f32[3,1,128]{2,0,1:T(4,128)S(1)} %get-tuple-element.16), channel_id=1, source_target_pairs={{16,0},{32,16},{48,32},{64,48},{80,64},{96,80},{112,96},{128,112},... | collective-permute-start | bytes 4616 | tf_op jit(solution)/shard_map/ppermute | solution.py:22
  82.0 3.1 collective-permute-start.9
  85.2 3.0 collective-permute-start.11
  86.8 4.7 %collective-permute-start.12 = (f32[3,18,1]{2,0,1:T(4,128)S(1)}, f32[3,18,1]{2,0,1:T(4,128)S(1)}, u32[]{:S(2)}, u32[]{:S(2)}) collective-permute-start(f32[3,18,1]{2,0,1:T(4,128)S(1)} %get-tuple-element.9), channel_id=1, source_target_pairs={{1,0},{2,1},{3,2},{4,3},{5,4},{6,5},{7,6},{8,7},{9,8},{10,9},{11,1... | collective-permute-start | bytes 656 | tf_op jit(solution)/shard_map/ppermute | solution.py:22
  91.7 0.7 copy-start.5
  183.4 105.9 %copy-start.18 = (f32[2]{0:T(128)}, f32[2]{0:T(128)S(1)}, u32[]{:S(2)}) copy-start(f32[2]{0:T(128)S(1)} %psum.29) | copy-start | bytes 28
  289.3 0.6 copy-start.16
  290.7 4.6 collective-permute-start.13
  295.6 5.2 %collective-permute-start.14 = (f32[2,128]{1,0:T(2,128)S(1)}, f32[2,128]{1,0:T(2,128)S(1)}, u32[]{:S(2)}, u32[]{:S(2)}) collective-permute-start(f32[2,128]{1,0:T(2,128)S(1)} %fusion.82), channel_id=1, source_target_pairs={{0,2},{1,3},{2,0},{3,1},{4,6},{5,7},{6,4},{7,5},{8,10},{9,11},{10,... | collective-permute-start | bytes 3080 | tf_op jit(solution)/shard_map/ppermute | solution.py:32
  300.9 8.2 %collective-permute-start.15 = (f32[2,128]{1,0:T(2,128)S(1)}, f32[2,128]{1,0:T(2,128)S(1)}, u32[]{:S(2)}, u32[]{:S(2)}) collective-permute-start(f32[2,128]{1,0:T(2,128)S(1)} %fusion.74), channel_id=1, source_target_pairs={{0,4},{1,5},{2,6},{3,7},{4,0},{5,1},{6,2},{7,3},{8,12},{9,13},{10,... | collective-permute-start | bytes 3080 | tf_op jit(solution)/shard_map/ppermute | solution.py:32
  309.3 13.0 %collective-permute-start.16 = (f32[2,128]{1,0:T(2,128)S(1)}, f32[2,128]{1,0:T(2,128)S(1)}, u32[]{:S(2)}, u32[]{:S(2)}) collective-permute-start(f32[2,128]{1,0:T(2,128)S(1)} %fusion.66), channel_id=1, source_target_pairs={{0,8},{1,9},{2,10},{3,11},{4,12},{5,13},{6,14},{7,15},{8,0},{9,1},... | collective-permute-start | bytes 3080 | tf_op jit(solution)/shard_map/ppermute | solution.py:32
  322.3 0.6 copy-start.8
  322.9 7.7 %collective-permute-start.17 = (f32[2,128]{1,0:T(2,128)S(1)}, f32[2,128]{1,0:T(2,128)S(1)}, u32[]{:S(2)}, u32[]{:S(2)}) collective-permute-start(f32[2,128]{1,0:T(2,128)S(1)} %fusion.58), channel_id=1, source_target_pairs={{0,16},{1,17},{2,18},{3,19},{4,20},{5,21},{6,22},{7,23},{8,24},{9,... | collective-permute-start | bytes 3080 | tf_op jit(solution)/shard_map/ppermute | solution.py:32
  330.6 0.6 copy-start.10
  331.2 4.3 collective-permute-start.18
  335.5 0.6 copy-start.12
  336.1 5.8 %collective-permute-start.19 = (f32[2,128]{1,0:T(2,128)S(1)}, f32[2,128]{1,0:T(2,128)S(1)}, u32[]{:S(2)}, u32[]{:S(2)}) collective-permute-start(f32[2,128]{1,0:T(2,128)S(1)} %fusion.42), channel_id=1, source_target_pairs={{0,64},{1,65},{2,66},{3,67},{4,68},{5,69},{6,70},{7,71},{8,72},{9,... | collective-permute-start | bytes 3080 | tf_op jit(solution)/shard_map/ppermute | solution.py:32
  341.9 0.6 copy-start.14
  342.4 4.4 collective-permute-start.20
  347.6 7.0 %collective-permute-start.21 = (f32[2,128]{1,0:T(2,128)S(1)}, f32[2,128]{1,0:T(2,128)S(1)}, u32[]{:S(2)}, u32[]{:S(2)}) collective-permute-start(f32[2,128]{1,0:T(2,128)S(1)} %fusion.26), channel_id=1, source_target_pairs={{0,256},{1,257},{2,258},{3,259},{4,260},{5,261},{6,262},{7,263},{8... | collective-permute-start | bytes 3080 | tf_op jit(solution)/shard_map/ppermute | solution.py:32
  355.9 0.7 copy-start.15
  356.7 0.7 copy-start.13
  357.6 0.7 copy-start.11
  358.4 0.7 copy-start.9
  361.9 104.7 %copy-start.19 = (f32[2]{0:T(128)S(1)}, f32[2]{0:T(128)}, u32[]{:S(2)}) copy-start(f32[2]{0:T(128)} %copy-done.18) | copy-start | bytes 28
  466.6 0.7 copy-start.17
